TPU v7x, 512 devices: a whole 4x8x8 slice. The times are simulated.
512 devices in a mesh: slab: 16 (over y_lo, z), group: 32 (over x, y_hi, core).
Axes of the slice: x: 4, y: 8 (y_hi: 4, y_lo: 2; y = y_hi * 2 + y_lo), z: 8, core: 2. Of those that a mesh axis runs over, the one named last changes fastest.
Arguments:
- images: bfloat16 [131072, 768], P(('slab', 'group')), may hold values from -200 to 200
- references: bfloat16 [8192, 768], P(('slab', 'group')), may hold values from -4 to 4
- ctf_table: float32 [32, 384], replicated, may hold values from -1.3 to 1.3
- ctf_ids: int32 [131072], P(('slab', 'group')), may hold values from 0 to 31
- owners: int32 [131072], P(('slab', 'group')), may hold values from 0 to 15, as said below
Outputs:
- new_references: float32 [8192, 768], P(('slab', 'group'))
- log_evidence: float32 [131072], P(('slab', 'group'))
Inputs may be any that keep to these rules, and one draw needn't show every extreme that they name: `owners`: no slab is named by more than 48 lines of one device's 256, and in every device's lines one slab is named by exactly 48.
All inputs are finite; a program needn't handle non-finite values.
Results may differ from a plain program's by a relative error of at most 0.003.
Values may be sent and summed in bfloat16 or wider, within the bound.
A program may use at most 64 MiB of HBM per device.

v0:
```python
import jax
import jax.numpy as jnp
from jax import lax
from jax.sharding import PartitionSpec as P


def slot_plan(owner_block, slab_count, capacity):
    line_count = owner_block.shape[0]
    one_hot = (owner_block[:, None] == jnp.arange(slab_count, dtype=jnp.int32)[None, :]).astype(
        jnp.int32
    )
    earlier = jnp.cumsum(one_hot, axis=0) - one_hot
    rank_index = jnp.sum(earlier * one_hot, axis=1)
    slot_index = owner_block * capacity + rank_index
    filled_slot = (
        jnp.zeros((slab_count * capacity,), jnp.int32)
        .at[slot_index]
        .set(jnp.arange(line_count, dtype=jnp.int32) + 1)
    )
    filled_mask = filled_slot > 0
    source_row = jnp.maximum(filled_slot - 1, 0)
    return (slot_index, source_row, filled_mask)


def weigh(image_slots, ctf_tags, ctf_table):
    group_count = ctf_table.shape[0]
    levels = jnp.arange(1, group_count + 1, dtype=jnp.float32)
    group_pick = (ctf_tags.astype(jnp.float32)[:, None] == levels[None, :]).astype(jnp.float32)
    ctf_rows = jnp.dot(group_pick, ctf_table, precision=lax.Precision.HIGHEST)
    weighted = (
        image_slots.astype(jnp.float32) * jnp.concatenate([ctf_rows, ctf_rows], axis=1)
    ).astype(jnp.bfloat16)
    ctf_square = (ctf_rows * ctf_rows).astype(jnp.bfloat16)
    return (weighted, ctf_square)


def score_block(weighted, ctf_square, ref_lines):
    half_width = ref_lines.shape[1] // 2
    widened = ref_lines.astype(jnp.float32)
    line_power = (widened[:, :half_width] ** 2 + widened[:, half_width:] ** 2).astype(jnp.bfloat16)
    cross_term = lax.dot_general(
        weighted, ref_lines, (((1,), (1,)), ((), ())), preferred_element_type=jnp.float32
    )
    quad_term = lax.dot_general(
        ctf_square, line_power, (((1,), (1,)), ((), ())), preferred_element_type=jnp.float32
    )
    return (cross_term - 0.5 * quad_term) * ref_lines.shape[1] ** (-0.5)


def on_device(images, references, ctf_table, ctf_ids, owners):
    slab_count = lax.axis_size("slab")
    line_count = images.shape[0]
    capacity = 3 * line_count // slab_count
    slot_index, source_row, filled_mask = slot_plan(owners, slab_count, capacity)
    image_slots = jnp.where(filled_mask[:, None], images[source_row], jnp.zeros((), jnp.bfloat16))
    ctf_tags = jnp.where(filled_mask, ctf_ids[source_row] + 1, 0).astype(jnp.bfloat16)
    arrived_lines, arrived_tags = (
        lax.all_to_all(image_slots, "slab", split_axis=0, concat_axis=0, tiled=True),
        lax.all_to_all(ctf_tags, "slab", split_axis=0, concat_axis=0, tiled=True),
    )
    weighted, ctf_square = weigh(arrived_lines, arrived_tags, ctf_table)
    arrived_mask = arrived_tags.astype(jnp.float32) > 0.0
    scores = score_block(
        weighted, ctf_square, lax.all_gather(references, "group", axis=0, tiled=True)
    )
    score_max = jnp.max(scores, axis=1, keepdims=True)
    exp_total = jnp.sum(jnp.exp(scores - score_max), axis=1, keepdims=True)
    evidence = score_max + jnp.log(exp_total)
    responsibility = (
        jnp.exp(scores - evidence) * arrived_mask[:, None].astype(jnp.float32)
    ).astype(jnp.bfloat16)
    numerator = lax.dot_general(
        responsibility, weighted, (((0,), (0,)), ((), ())), preferred_element_type=jnp.float32
    )
    denominator = lax.dot_general(
        responsibility, ctf_square, (((0,), (0,)), ((), ())), preferred_element_type=jnp.float32
    )
    returned = lax.all_to_all(evidence[:, 0], "slab", split_axis=0, concat_axis=0, tiled=True)
    line_evidence = returned[slot_index]
    summed_num, summed_den = lax.psum((numerator, denominator), "group")
    share_rows = numerator.shape[0] // lax.axis_size("group")
    offset = lax.axis_index("group") * share_rows
    share_num = lax.dynamic_slice_in_dim(summed_num, offset, share_rows, 0)
    share_den = lax.dynamic_slice_in_dim(summed_den, offset, share_rows, 0)
    new_references = share_num / (jnp.concatenate([share_den, share_den], axis=1) + 1.0)
    return (new_references, line_evidence)


def solution(mesh):
    in_specs = (
        P(("slab", "group"), None),
        P(("slab", "group"), None),
        P(),
        P(("slab", "group")),
        P(("slab", "group")),
    )
    out_specs = (P(("slab", "group"), None), P(("slab", "group")))
    return jax.shard_map(
        on_device, mesh=mesh, in_specs=in_specs, out_specs=out_specs, check_vma=False
    )
```

profile of v0, /device:TPU:1, one launch (start us, length us, event | category | flops | bytes accessed | tf_op | source)
XLA Modules:
  0.0 413.9 jit_solution(3139050886746585395)
XLA Ops:
  7.2 0.7 fusion.14
  8.7 0.8 fusion.13
  10.2 1.4 scatter_custom_fusion
  11.6 5.0 %gather_fusion.1 = s32[768]{0:T(1024)S(1)} fusion(s32[256]{0:T(256)S(1)} %copy-done.1, s32[1024]{0:T(1024)S(1)} %pad_clamp_fusion.1), kind=kCustom, calls=%fused_computation.1 | custom fusion | bytes 9216 | tf_op jit(solution)/shard_map/gather | solution.py:56
  17.3 12.0 %all-to-all-start.1 = ((bf16[16,48,1]{1,2,0:T(2,128)(2,1)}), bf16[16,48,1]{1,2,0:T(2,128)(2,1)S(1)}, u32[]{:S(2)}, u32[]{:S(2)}) async-start(bf16[16,48,1]{1,2,0:T(2,128)(2,1)} %all_to_all.21), calls=%async_computation.1 | async-start | bytes 16384 | tf_op jit(solution)/shard_map/all_to_all | solution.py:59
  29.4 2.8 gather_fusion
  32.2 1.2 broadcast_select_fusion
  33.4 3.2 all-to-all-done.1
  36.5 4.5 %all-to-all-start = ((bf16[16,48,768]{2,1,0:T(8,128)(2,1)}), bf16[16,48,768]{2,1,0:T(8,128)(2,1)S(1)}, u32[]{:S(2)}, u32[]{:S(2)}) async-start(bf16[16,48,768]{2,1,0:T(8,128)(2,1)} %broadcast_select_fusion), calls=%async_computation | async-start | bytes 2359296 | tf_op jit(solution)/shard_map/all_to_all | solution.py:58
  41.1 56.4 %all_gather.3 = bf16[512,768]{1,0:T(8,128)(2,1)S(1)} all-gather(bf16[16,768]{1,0:T(8,128)(2,1)S(1)} %copy-done.4), channel_id=1, replica_groups=mesh['slab'=16,'group'=32] {'group'}, dimensions={0}, use_global_device_ids=true | all-gather | bytes 811008 | tf_op jit(solution)/shard_map/all_gather | solution.py:64
  97.5 1.3 convert_element_type.63
  99.4 1.6 fusion.4
  101.1 1.6 bitcast_convert_fusion
  102.7 3.1 copy.12
  105.8 2.7 fusion.18
  109.4 0.8 copy-done.2
  110.1 2.1 fusion.9
  112.2 1.5 fusion.6
  114.4 7.5 %all-to-all-start.2 = ((f32[16,48,1]{1,2,0:T(1,128)}), f32[16,48,1]{1,2,0:T(1,128)S(1)}, u32[]{:S(2)}, u32[]{:S(2)}) async-start(f32[16,48,1]{1,2,0:T(1,128)} %bitcast.4), calls=%async_computation.2 | async-start | bytes 16384 | tf_op jit(solution)/shard_map/all_to_all | solution.py:78
  122.0 7.3 %all-to-all-done.2 = f32[16,48,1]{1,2,0:T(1,128)S(1)} async-done(((f32[16,48,1]{1,2,0:T(1,128)}), f32[16,48,1]{1,2,0:T(1,128)S(1)}, u32[]{:S(2)}, u32[]{:S(2)}) %all-to-all-start.2) | async-done | bytes 3104 | tf_op jit(solution)/shard_map/all_to_all | solution.py:78
  130.6 1.9 gather_fusion.2
  132.5 272.4 %all-reduce.3.cloned.1.call-done = (f32[512,384]{1,0:T(8,128)}, f32[512,768]{1,0:T(8,128)}) async-done(((f32[512,384]{1,0:T(8,128)}, f32[512,768]{1,0:T(8,128)}), (f32[512,384]{1,0:T(8,128)}, f32[512,768]{1,0:T(8,128)})) %all-reduce.3.cloned.1.call-update) | async-done | bytes 2359312 | tf_op jit(solution)/shard_map/psum | solution.py:80
  404.9 0.7 constant_dynamic-slice_fusion
  405.6 1.4 fusion.10
  (34 shorter events, 5.8 us)
Async XLA Ops:
  7.2 22.2 %copy-start = (bf16[256,768]{1,0:T(8,128)(2,1)S(1)}, bf16[256,768]{1,0:T(8,128)(2,1)}, u32[]{:S(2)}) copy-start(bf16[256,768]{1,0:T(8,128)(2,1)} %param.5) | copy-start | bytes 1179652
  7.2 4.4 %copy-start.1 = (s32[256]{0:T(256)S(1)}, s32[256]{0:T(256)}, u32[]{:S(2)}) copy-start(s32[256]{0:T(256)} %param.8) | copy-start | bytes 3076
  17.3 19.2 %all-to-all-start.1 = ((bf16[16,48,1]{1,2,0:T(2,128)(2,1)}), bf16[16,48,1]{1,2,0:T(2,128)(2,1)S(1)}, u32[]{:S(2)}, u32[]{:S(2)}) async-start(bf16[16,48,1]{1,2,0:T(2,128)(2,1)} %all_to_all.21), calls=%async_computation.1 | async-start | bytes 16384 | tf_op jit(solution)/shard_map/all_to_all | solution.py:59
  33.4 7.8 %copy-start.4 = (bf16[16,768]{1,0:T(8,128)(2,1)S(1)}, bf16[16,768]{1,0:T(8,128)(2,1)}, u32[]{:S(2)}) copy-start(bf16[16,768]{1,0:T(8,128)(2,1)} %param.6) | copy-start | bytes 73732
  36.5 64.5 %all-to-all-start = ((bf16[16,48,768]{2,1,0:T(8,128)(2,1)}), bf16[16,48,768]{2,1,0:T(8,128)(2,1)S(1)}, u32[]{:S(2)}, u32[]{:S(2)}) async-start(bf16[16,48,768]{2,1,0:T(8,128)(2,1)} %broadcast_select_fusion), calls=%async_computation | async-start | bytes 2359296 | tf_op jit(solution)/shard_map/all_to_all | solution.py:58
  41.1 363.8 %all-reduce.3.cloned.1.call-start = ((), (), s32[]{:S(2)}) async-start(), calls=%async_computation.3 | async-start | bytes 4718592 | tf_op jit(solution)/shard_map/psum | solution.py:80
  105.8 2.7 copy-start.3
  108.5 1.7 copy-start.2
  114.4 14.9 %all-to-all-start.2 = ((f32[16,48,1]{1,2,0:T(1,128)}), f32[16,48,1]{1,2,0:T(1,128)S(1)}, u32[]{:S(2)}, u32[]{:S(2)}) async-start(f32[16,48,1]{1,2,0:T(1,128)} %bitcast.4), calls=%async_computation.2 | async-start | bytes 16384 | tf_op jit(solution)/shard_map/all_to_all | solution.py:78
Sparse Core Ops, SparseCore 0:
  113.9 290.9 all-reduce.2
where the time goes:
time: 415 us; the launch traced here: 414 us
  waiting for transfers between devices  283 us (68%)
  blocking collectives  56.4 us (14%)
  starting transfers between devices  24 us (6%)
  local copies, waits for them, and re-layouts  18 us (4%)
  between operations  14.2 us (3%)
  other arithmetic  9.84 us (2%)
  matrix products  8.53 us (2%)
    psum x1, waiting for transfers between devices, on_device(): summed_num, summed_den = lax.psum((numerator, denominator), 'group')  272 us
    all_gather x1, blocking collectives, on_device(): lax.all_gather(references, 'group', axis=0, tiled=True)  56.4 us
    all_to_all x1, starting transfers between devices, on_device(): lax.all_to_all(ctf_tags, 'slab', split_axis=0, concat_axis=0, tiled=True)  12 us
  transfers between devices with their start and end apart: 4, of which 3 were waited for; matrix products, arithmetic and copies ran while one was open for 3% of the time, Pallas kernels for 0%

commit v1 on v0

--- a/solution.py
+++ b/solution.py
@@ -61,7 +61,11 @@
     weighted, ctf_square = weigh(arrived_lines, arrived_tags, ctf_table)
     arrived_mask = arrived_tags.astype(jnp.float32) > 0.0
     scores = score_block(
-        weighted, ctf_square, lax.all_gather(references, "group", axis=0, tiled=True)
+        weighted,
+        ctf_square,
+        jnp.concatenate(
+            lax.all_to_all(jnp.stack([references] * lax.axis_size("group")), "group", 0, 0), axis=0
+        ),
     )
     score_max = jnp.max(scores, axis=1, keepdims=True)
     exp_total = jnp.sum(jnp.exp(scores - score_max), axis=1, keepdims=True)

time: 415 us -> 412 us (level)
  waiting for transfers between devices: 283 us -> 327 us
  blocking collectives: 56.4 us -> 19.1 us
    all_gather x1 -> x0, blocking collectives: 56.4 us -> none  [on_device(): lax.all_gather(references, 'group', axis=0, tiled=True)]
    all_to_all x1, waiting for transfers between devices: 0.01 us -> 25.2 us  [on_device(): lax.all_to_all(image_slots, 'slab', split_axis=0, concat_axis=0, tiled=True)]
    all_to_all x0 -> x1, blocking collectives: none -> 19.1 us  [on_device(): lax.all_to_all(ctf_tags, 'slab', split_axis=0, concat_axis=0, tiled=True)]
    all_to_all x1, waiting for transfers between devices: 3.18 us -> 19 us  [on_device(): lax.all_to_all(jnp.stack([references] * lax.axis_size('group')), 'group',...]
  transfers between devices with their start and end apart: 4 -> 4, of which waited for: 3 -> 4; matrix products, arithmetic and copies ran while one was open for 3% -> 3% of each run, Pallas kernels for 0% -> 0%
where the time goes in v1:
time: 412 us
  waiting for transfers between devices  327 us (79%)
  starting transfers between devices  21.5 us (5%)
  blocking collectives  19.1 us (5%)
  local copies, waits for them, and re-layouts  15 us (4%)
  between operations  14.2 us (3%)
  other arithmetic  8.18 us (2%)
  matrix products  6.36 us (2%)
    psum x1, waiting for transfers between devices, on_device(): summed_num, summed_den = lax.psum((numerator, denominator), 'group')  276 us
    all_to_all x1, waiting for transfers between devices, on_device(): lax.all_to_all(image_slots, 'slab', split_axis=0, concat_axis=0, tiled=True)  25.2 us
    all_to_all x1, blocking collectives, on_device(): lax.all_to_all(ctf_tags, 'slab', split_axis=0, concat_axis=0, tiled=True)  19.1 us
    all_to_all x1, waiting for transfers between devices, on_device(): lax.all_to_all(jnp.stack([references] * lax.axis_size('group')), 'group',...  19 us
    all_to_all x1, starting transfers between devices, on_device(): lax.all_to_all(jnp.stack([references] * lax.axis_size('group')), 'group',...  10.9 us
  transfers between devices with their start and end apart: 4, of which 4 were waited for; matrix products, arithmetic and copies ran while one was open for 3% of the time, Pallas kernels for 0%

profile of v1, /device:TPU:1, one launch (start us, length us, event | category | flops | bytes accessed | tf_op | source)
XLA Modules:
  0.0 411.8 jit_solution(14866728140728733923)
XLA Ops:
  7.2 0.7 fusion.15
  8.7 0.8 fusion.14
  9.5 0.7 compare_select_fusion
  10.2 1.4 scatter_custom_fusion
  11.6 5.0 %gather_fusion.1 = s32[768]{0:T(1024)S(1)} fusion(s32[256]{0:T(256)S(1)} %copy-done.1, s32[1024]{0:T(1024)S(1)} %pad_clamp_fusion.1), kind=kCustom, calls=%fused_computation.1 | custom fusion | bytes 9216 | tf_op jit(solution)/shard_map/gather | solution.py:56
  16.7 19.1 %all_to_all.30 = bf16[16,48,1]{1,2,0:T(2,128)(2,1)S(1)} all-to-all(bf16[16,48,1]{1,2,0:T(2,128)(2,1)S(1)} %all_to_all.25), channel_id=1, replica_groups=mesh['slab'=16,'group'=32] {'slab'}, dimensions={0} | all-to-all | bytes 3072 | tf_op jit(solution)/shard_map/all_to_all | solution.py:59
  35.8 0.9 stack.2
  36.7 10.9 %all-to-all-start.2 = ((bf16[32,16,768]{2,1,0:T(8,128)(2,1)}), bf16[32,16,768]{2,1,0:T(8,128)(2,1)S(1)}, u32[]{:S(2)}, u32[]{:S(2)}) async-start(bf16[32,16,768]{2,1,0:T(8,128)(2,1)} %stack.2), calls=%async_computation.2 | async-start | bytes 1572864 | tf_op jit(solution)/shard_map/all_to_all | solution.py:67
  47.8 2.8 gather_fusion
  50.5 1.2 broadcast_select_fusion
  51.7 19.0 %all-to-all-done.2 = bf16[32,16,768]{2,1,0:T(8,128)(2,1)S(1)} async-done(((bf16[32,16,768]{2,1,0:T(8,128)(2,1)}), bf16[32,16,768]{2,1,0:T(8,128)(2,1)S(1)}, u32[]{:S(2)}, u32[]{:S(2)}) %all-to-all-start.2) | async-done | bytes 786464 | tf_op jit(solution)/shard_map/all_to_all | solution.py:67
  70.8 3.7 all-to-all-start
  74.7 1.5 fusion.5
  76.1 1.3 bitcast_convert_fusion
  77.4 25.2 %all-to-all-done = bf16[16,48,768]{2,1,0:T(8,128)(2,1)S(1)} async-done(((bf16[16,48,768]{2,1,0:T(8,128)(2,1)}), bf16[16,48,768]{2,1,0:T(8,128)(2,1)S(1)}, u32[]{:S(2)}, u32[]{:S(2)}) %all-to-all-start) | async-done | bytes 1179680 | tf_op jit(solution)/shard_map/all_to_all | solution.py:58
  102.9 0.8 fusion.19
  105.2 1.5 fusion.7
  106.9 2.0 fusion.10
  109.6 6.8 %all-to-all-start.3 = ((f32[16,48,1]{1,2,0:T(1,128)}), f32[16,48,1]{1,2,0:T(1,128)S(1)}, u32[]{:S(2)}, u32[]{:S(2)}) async-start(f32[16,48,1]{1,2,0:T(1,128)} %bitcast.7), calls=%async_computation.3 | async-start | bytes 16384 | tf_op jit(solution)/shard_map/all_to_all | solution.py:82
  116.4 7.2 %all-to-all-done.3 = f32[16,48,1]{1,2,0:T(1,128)S(1)} async-done(((f32[16,48,1]{1,2,0:T(1,128)}), f32[16,48,1]{1,2,0:T(1,128)S(1)}, u32[]{:S(2)}, u32[]{:S(2)}) %all-to-all-start.3) | async-done | bytes 3104 | tf_op jit(solution)/shard_map/all_to_all | solution.py:82
  124.9 1.9 gather_fusion.2
  126.8 276.0 %all-reduce.3.cloned.1.call-done = (f32[512,384]{1,0:T(8,128)}, f32[512,768]{1,0:T(8,128)}) async-done(((f32[512,384]{1,0:T(8,128)}, f32[512,768]{1,0:T(8,128)}), (f32[512,384]{1,0:T(8,128)}, f32[512,768]{1,0:T(8,128)})) %all-reduce.3.cloned.1.call-update) | async-done | bytes 2359312 | tf_op jit(solution)/shard_map/psum | solution.py:84
  402.8 0.7 constant_dynamic-slice_fusion
  403.5 1.4 fusion.11
  (33 shorter events, 5.0 us)
Async XLA Ops:
  7.2 40.6 %copy-start = (bf16[256,768]{1,0:T(8,128)(2,1)S(1)}, bf16[256,768]{1,0:T(8,128)(2,1)}, u32[]{:S(2)}) copy-start(bf16[256,768]{1,0:T(8,128)(2,1)} %param.5) | copy-start | bytes 1179652
  7.2 4.4 %copy-start.1 = (s32[256]{0:T(256)S(1)}, s32[256]{0:T(256)}, u32[]{:S(2)}) copy-start(s32[256]{0:T(256)} %param.8) | copy-start | bytes 3076
  11.6 24.2 %copy-start.3 = (bf16[16,768]{1,0:T(8,128)(2,1)S(1)}, bf16[16,768]{1,0:T(8,128)(2,1)}, u32[]{:S(2)}) copy-start(bf16[16,768]{1,0:T(8,128)(2,1)} %param.6) | copy-start | bytes 73732
  36.7 34.0 %all-to-all-start.2 = ((bf16[32,16,768]{2,1,0:T(8,128)(2,1)}), bf16[32,16,768]{2,1,0:T(8,128)(2,1)S(1)}, u32[]{:S(2)}, u32[]{:S(2)}) async-start(bf16[32,16,768]{2,1,0:T(8,128)(2,1)} %stack.2), calls=%async_computation.2 | async-start | bytes 1572864 | tf_op jit(solution)/shard_map/all_to_all | solution.py:67
  70.8 31.9 %all-to-all-start = ((bf16[16,48,768]{2,1,0:T(8,128)(2,1)}), bf16[16,48,768]{2,1,0:T(8,128)(2,1)S(1)}, u32[]{:S(2)}, u32[]{:S(2)}) async-start(bf16[16,48,768]{2,1,0:T(8,128)(2,1)} %broadcast_select_fusion), calls=%async_computation | async-start | bytes 2359296 | tf_op jit(solution)/shard_map/all_to_all | solution.py:58
  74.5 328.3 %all-reduce.3.cloned.1.call-start = ((), (), s32[]{:S(2)}) async-start(), calls=%async_computation.4 | async-start | bytes 4718592 | tf_op jit(solution)/shard_map/psum | solution.py:84
  102.9 1.4 copy-start.2
  109.6 14.0 %all-to-all-start.3 = ((f32[16,48,1]{1,2,0:T(1,128)}), f32[16,48,1]{1,2,0:T(1,128)S(1)}, u32[]{:S(2)}, u32[]{:S(2)}) async-start(f32[16,48,1]{1,2,0:T(1,128)} %bitcast.7), calls=%async_computation.3 | async-start | bytes 16384 | tf_op jit(solution)/shard_map/all_to_all | solution.py:82
Sparse Core Ops, SparseCore 0:
  109.0 293.7 all-reduce.2
